TPU v7x, 128 devices: a whole 4x4x4 slice. The times are simulated.
128 devices in a mesh: row: 8 (over y_lo, z), col: 16 (over x, y_hi, core).
Axes of the slice: x: 4, y: 4 (y_hi: 2, y_lo: 2; y = y_hi * 2 + y_lo), z: 4, core: 2. Of those that a mesh axis runs over, the one named last changes fastest.
Arguments:
- inputs: bfloat16 [1024, 8192], P('col', 'row'), may hold values from -6 to 6
- cotangent: bfloat16 [1024, 8192], P('col', 'row'), may hold values from -6 to 6
- gate_weight: bfloat16 [8192, 14336], P('row', 'col'), may hold values from -0.0625 to 0.0625
- up_weight: bfloat16 [8192, 14336], P('row', 'col'), may hold values from -0.0625 to 0.0625
- down_weight: bfloat16 [14336, 8192], P('col', 'row'), may hold values from -0.046875 to 0.046875
Outputs:
- input_grad: bfloat16 [1024, 8192], P('col', 'row')
- gate_grad: bfloat16 [8192, 14336], P('row', 'col')
- up_grad: bfloat16 [8192, 14336], P('row', 'col')
- down_grad: bfloat16 [14336, 8192], P('col', 'row')
All inputs are finite; a program needn't handle non-finite values.
Results may differ from a plain program's by a relative error of at most 0.005.
Values may be sent and summed in bfloat16 or wider, within the bound.
A program may use at most 128 MiB of HBM per device.

v0:
```python
import jax
import jax.numpy as jnp
from jax import lax
from jax.sharding import PartitionSpec as P


def dot_last(left, right):
    return lax.dot_general(
        left, right, (((1,), (1,)), ((), ())), preferred_element_type=jnp.float32
    )


def dot_first(left, right):
    return lax.dot_general(
        left, right, (((0,), (0,)), ((), ())), preferred_element_type=jnp.float32
    )


def shards(inputs, cotangent, gate_weight, up_weight, down_weight):
    inputs_all, cot_all = (
        lax.all_gather(inputs, "col", axis=0, tiled=True),
        lax.all_gather(cotangent, "col", axis=0, tiled=True),
    )
    hid_cols = gate_weight.shape[1]
    gate_part = jnp.dot(inputs_all, gate_weight, preferred_element_type=jnp.float32)
    up_part = jnp.dot(inputs_all, up_weight, preferred_element_type=jnp.float32)
    summed = lax.psum_scatter(
        jnp.concatenate([gate_part, up_part], axis=1), "row", scatter_dimension=0, tiled=True
    )
    gate = summed[:, :hid_cols]
    up = summed[:, hid_cols:]
    slope = lax.psum_scatter(dot_last(cot_all, down_weight), "row", scatter_dimension=0, tiled=True)
    sig = jax.nn.sigmoid(gate)
    act = gate * sig
    deriv = sig * (1.0 + gate * (1.0 - sig))
    hidden = (act * up).astype(jnp.bfloat16)
    gate_delta = (slope * up * deriv).astype(jnp.bfloat16)
    up_delta = (slope * act).astype(jnp.bfloat16)
    hidden_all, gdelta_all, udelta_all = (
        lax.all_gather(hidden, "row", axis=0, tiled=True),
        lax.all_gather(gate_delta, "row", axis=0, tiled=True),
        lax.all_gather(up_delta, "row", axis=0, tiled=True),
    )
    down_grad = dot_first(hidden_all, cot_all).astype(jnp.bfloat16)
    gate_grad = dot_first(inputs_all, gdelta_all).astype(jnp.bfloat16)
    up_grad = dot_first(inputs_all, udelta_all).astype(jnp.bfloat16)
    input_grad = lax.psum_scatter(
        dot_last(gdelta_all, gate_weight) + dot_last(udelta_all, up_weight),
        "col",
        scatter_dimension=0,
        tiled=True,
    ).astype(jnp.bfloat16)
    return (input_grad, gate_grad, up_grad, down_grad)


def solution(mesh):
    placed = (P("col", "row"), P("col", "row"), P("row", "col"), P("row", "col"), P("col", "row"))
    return jax.shard_map(
        shards,
        mesh=mesh,
        in_specs=placed,
        out_specs=(P("col", "row"), P("row", "col"), P("row", "col"), P("col", "row")),
        check_vma=False,
    )
```

profile of v0, /device:TPU:0, one launch (start us, length us, event | category | flops | bytes accessed | tf_op | source)
XLA Modules:
  0.0 465.0 jit_solution(12848100826845853382)
XLA Ops:
  7.2 0.7 all-gather.6.cloned.1.call-update
  8.0 0.7 all-gather.8.cloned.1.call-update
  8.7 52.5 %all-gather.6.cloned.1.call-done = bf16[1024,1024]{1,0:T(8,128)(2,1)} async-done(((bf16[64,1024]{1,0:T(8,128)(2,1)}), bf16[1024,1024]{1,0:T(8,128)(2,1)}) %all-gather.6.cloned.1.call-update) | async-done | bytes 2097168 | tf_op jit(solution)/shard_map/all_gather | solution.py:22
  61.2 6.4 %fusion.1 = f32[1024,896]{1,0:T(8,128)} fusion(bf16[1024,1024]{1,0:T(8,128)(2,1)} %all-gather.6.cloned.1.call-done, bf16[896,1024]{1,0:T(8,128)(2,1)} %param.9), kind=kOutput, calls=%fused_computation.10 | convolution fusion | flops 1879048192 | bytes 7602176 | tf_op jit(solution)/shard_map/dot_general | solution.py:8
  67.7 43.1 %all-gather.8.cloned.1.call-done = bf16[1024,1024]{1,0:T(8,128)(2,1)} async-done(((bf16[64,1024]{1,0:T(8,128)(2,1)}), bf16[1024,1024]{1,0:T(8,128)(2,1)}) %all-gather.8.cloned.1.call-update) | async-done | bytes 2097168 | tf_op jit(solution)/shard_map/all_gather | solution.py:21
  110.9 4.1 fusion.2
  114.9 2.3 fusion.3
  117.3 3.5 pad_maximum_fusion
  120.9 40.3 %reduce-scatter.4.cloned.1.call-done = f32[128,896]{1,0:T(8,128)} async-done(((f32[1024,896]{1,0:T(8,128)}), f32[128,896]{1,0:T(8,128)}) %reduce-scatter.4.cloned.1.call-update) | async-done | bytes 458768 | tf_op jit(solution)/shard_map/reduce_scatter | solution.py:32
  161.2 84.6 %reduce-scatter.6.cloned.1.call-done = f32[128,1792]{1,0:T(8,128)} async-done(((f32[1024,1792]{1,0:T(8,128)}), f32[128,1792]{1,0:T(8,128)}) %reduce-scatter.6.cloned.1.call-update) | async-done | bytes 917520 | tf_op jit(solution)/shard_map/reduce_scatter | solution.py:27
  245.8 2.3 multiply_convert_fusion.1
  248.8 0.7 all-gather.14.cloned.1.call-update
  249.7 38.4 %all-gather.10.cloned.1.call-done = bf16[1024,896]{1,0:T(8,128)(2,1)} async-done(((bf16[128,896]{1,0:T(8,128)(2,1)}), bf16[1024,896]{1,0:T(8,128)(2,1)}) %all-gather.10.cloned.1.call-update) | async-done | bytes 1835024 | tf_op jit(solution)/shard_map/all_gather | solution.py:41
  288.1 5.8 %fusion.4 = f32[1024,1024]{1,0:T(8,128)} fusion(bf16[1024,896]{1,0:T(8,128)(2,1)} %all-gather.10.cloned.1.call-done, bf16[1024,896]{1,0:T(8,128)(2,1)S(1)} %copy-done), kind=kOutput, calls=%fused_computation.13 | convolution fusion | flops 1879048192 | bytes 7864320 | tf_op jit(solution)/shard_map/dot_general | solution.py:8
  293.9 36.7 %all-gather.12.cloned.1.call-done = bf16[1024,896]{1,0:T(8,128)(2,1)} async-done(((bf16[128,896]{1,0:T(8,128)(2,1)}), bf16[1024,896]{1,0:T(8,128)(2,1)}) %all-gather.12.cloned.1.call-update) | async-done | bytes 1835024 | tf_op jit(solution)/shard_map/all_gather | solution.py:42
  330.7 7.6 %convolution_add_fusion = f32[1024,1024]{1,0:T(8,128)} fusion(f32[1024,1024]{1,0:T(8,128)} %fusion.4, bf16[1024,896]{1,0:T(8,128)(2,1)} %all-gather.12.cloned.1.call-done, bf16[1024,896]{1,0:T(8,128)(2,1)} %param.8), kind=kOutput, calls=%fused_computation.1 | convolution fusion | flops 1880096768 | bytes 12058624 | tf_op jit(solution)/shard_map/dot_general | solution.py:8
  338.3 5.5 %convert_bitcast_fusion.1 = bf16[1024,896]{0,1:T(8,128)(2,1)} fusion(bf16[1024,896]{1,0:T(8,128)(2,1)} %all-gather.10.cloned.1.call-done, bf16[1024,1024]{1,0:T(8,128)(2,1)} %all-gather.8.cloned.1.call-done), kind=kOutput, calls=%fused_computation.3 | convolution fusion | flops 1879965696 | bytes 5767168 | tf_op jit(solution)/shard_map/dot_general | solution.py:14
  343.8 3.8 copy.11
  347.6 5.5 %convert_bitcast_fusion = bf16[1024,896]{0,1:T(8,128)(2,1)} fusion(bf16[1024,896]{1,0:T(8,128)(2,1)} %all-gather.12.cloned.1.call-done, bf16[1024,1024]{1,0:T(8,128)(2,1)} %all-gather.8.cloned.1.call-done), kind=kOutput, calls=%fused_computation.2 | convolution fusion | flops 1879965696 | bytes 5767168 | tf_op jit(solution)/shard_map/dot_general | solution.py:14
  353.1 3.8 copy.12
  356.9 15.9 %all-gather.14.cloned.1.call-done = bf16[1024,896]{1,0:T(8,128)(2,1)} async-done(((bf16[128,896]{1,0:T(8,128)(2,1)}), bf16[1024,896]{1,0:T(8,128)(2,1)}) %all-gather.14.cloned.1.call-update) | async-done | bytes 1835024 | tf_op jit(solution)/shard_map/all_gather | solution.py:40
  372.8 5.5 %convolution_convert_fusion = bf16[896,1024]{1,0:T(8,128)(2,1)} fusion(bf16[1024,896]{1,0:T(8,128)(2,1)} %all-gather.14.cloned.1.call-done, bf16[1024,1024]{1,0:T(8,128)(2,1)} %all-gather.6.cloned.1.call-done), kind=kOutput, calls=%fused_computation.4 | convolution fusion | flops 1879965696 | bytes 5767168 | tf_op jit(solution)/shard_map/dot_general | solution.py:14
  378.3 78.3 %reduce-scatter.8.cloned.1.call-done = f32[64,1024]{1,0:T(8,128)} async-done(((f32[1024,1024]{1,0:T(8,128)}), f32[64,1024]{1,0:T(8,128)}) %reduce-scatter.8.cloned.1.call-update) | async-done | bytes 262160 | tf_op jit(solution)/shard_map/reduce_scatter | solution.py:47
  456.6 1.6 convert_element_type.29
  (19 shorter events, 1.1 us)
Async XLA Ops:
  7.2 103.7 %copy-start = (bf16[1024,896]{1,0:T(8,128)(2,1)S(1)}, bf16[1024,896]{1,0:T(8,128)(2,1)}, u32[]{:S(2)}) copy-start(bf16[1024,896]{1,0:T(8,128)(2,1)} %param.7) | copy-start | bytes 5505028
  7.2 54.0 %all-gather.6.cloned.1.call-start = ((), (), s32[]{:S(2)}) async-start(), calls=%async_computation.3 | async-start | bytes 2228224 | tf_op jit(solution)/shard_map/all_gather | solution.py:22
  7.9 102.9 %all-gather.8.cloned.1.call-start = ((), (), s32[]{:S(2)}) async-start(), calls=%async_computation.5 | async-start | bytes 2228224 | tf_op jit(solution)/shard_map/all_gather | solution.py:21
  8.7 152.5 %reduce-scatter.4.cloned.1.call-start = ((), (), s32[]{:S(2)}) async-start(), calls=%async_computation.4 | async-start | bytes 4128768 | tf_op jit(solution)/shard_map/reduce_scatter | solution.py:32
  67.7 178.1 %reduce-scatter.6.cloned.1.call-start = ((), (), s32[]{:S(2)}) async-start(), calls=%async_computation.6 | async-start | bytes 8257536 | tf_op jit(solution)/shard_map/reduce_scatter | solution.py:27
  110.9 4.1 copy-start.1
  110.9 4.1 copy-start.2
  120.8 167.3 %all-gather.10.cloned.1.call-start = ((), (), s32[]{:S(2)}) async-start(), calls=%async_computation.7 | async-start | bytes 2064384 | tf_op jit(solution)/shard_map/all_gather | solution.py:41
  248.1 82.5 %all-gather.12.cloned.1.call-start = ((), (), s32[]{:S(2)}) async-start(), calls=%async_computation.8 | async-start | bytes 2064384 | tf_op jit(solution)/shard_map/all_gather | solution.py:42
  248.7 124.1 %all-gather.14.cloned.1.call-start = ((), (), s32[]{:S(2)}) async-start(), calls=%async_computation.10 | async-start | bytes 2064384 | tf_op jit(solution)/shard_map/all_gather | solution.py:40
  249.5 207.1 %reduce-scatter.8.cloned.1.call-start = ((), (), s32[]{:S(2)}) async-start(), calls=%async_computation.9 | async-start | bytes 4456448 | tf_op jit(solution)/shard_map/reduce_scatter | solution.py:47
Sparse Core Ops, SparseCore 0:
  10.4 50.7 all-gather.5
  63.6 47.1 all-gather.7
  113.3 47.8 reduce-scatter.3
  163.5 82.2 reduce-scatter.5
  248.2 39.8 all-gather.9
  290.2 40.4 all-gather.11
  332.3 40.4 all-gather.13
  376.9 79.6 reduce-scatter.7
where the time goes:
time: 465 us
  waiting for transfers between devices  393 us (85%)
  matrix products  42.7 us (9%)
  between operations  14.2 us (3%)
  local copies, waits for them, and re-layouts  7.61 us (2%)
  other arithmetic  7.48 us (2%)
    reduce_scatter x1, waiting for transfers between devices, shards(): lax.psum_scatter(jnp.concatenate([gate_part, up_part], axis=1), 'row', sc...  84.6 us
    reduce_scatter x1, waiting for transfers between devices, shards(): lax.psum_scatter(dot_last(gdelta_all, gate_weight) + dot_last(udelta_all,...  78.3 us
    all_gather x1, waiting for transfers between devices, shards(): lax.all_gather(cotangent, 'col', axis=0, tiled=True)  52.5 us
    all_gather x1, waiting for transfers between devices, shards(): lax.all_gather(inputs, 'col', axis=0, tiled=True)  43.1 us
    reduce_scatter x1, waiting for transfers between devices, shards(): lax.psum_scatter(dot_last(cot_all, down_weight), 'row', scatter_dimension...  40.3 us
    all_gather x1, waiting for transfers between devices, shards(): lax.all_gather(gate_delta, 'row', axis=0, tiled=True)  38.4 us
    all_gather x1, waiting for transfers between devices, shards(): lax.all_gather(up_delta, 'row', axis=0, tiled=True)  36.7 us
    dot_general x3, matrix products, dot_last(): lax.dot_general(left, right, (((1,), (1,)), ((), ())), preferred_element_...  19.8 us
  transfers between devices with their start and end apart: 8, of which 8 were waited for; matrix products, arithmetic and copies ran while one was open for 12% of the time, Pallas kernels for 0%

commit v1 on v0

v1 whole, which is shorter than its diff:
```python
import jax
import jax.numpy as jnp
from jax import lax
from jax.experimental import pallas as pl
from jax.experimental.pallas import tpu as pltpu
from jax.sharding import PartitionSpec as P

MESH = pl.DeviceIdType.MESH
F32, BF16 = jnp.float32, jnp.bfloat16
NB = 4
NZ, NY, NX, NH, NC = 4, 2, 4, 2, 2

ORDER = (
    "a1:0", "a2:0", "a1:1", "a2:1", "a1:2", "a3:0", "w:0", "s1:0", "a3:1", "s2:0", "a2:2", "s1:1", "s2:1",
    "a3:2", "s4:0", "a1:3", "s3:0", "s4:1", "s3:1", "s5:0", "s1:2", "a2:3", "s6a:0", "a3:3", "s5:1", "s1:3",
    "s2:2", "s2:3", "s6a:1", "s6b:0", "s4:2", "s4:3", "s6c:0", "s3:2", "s6c:1", "s3:3", "s5:2", "s7:0",
    "s8:0", "s6b:1", "s10:0", "s6a:2", "s5:3", "s8:1", "s6a:3", "s7:1", "s10:1", "s6c:2", "s6b:2", "s11:0",
    "s11:1", "s6c:3", "s6b:3", "s8:2", "s9:0", "s7:2", "s10:2", "s8:3", "s12:1", "s7:3", "s10:3", "s9:1",
    "s11:2", "s9:2", "g:0", "s11:3", "s9:3", "s12:0", "g:2", "g:3", "g:1", "s12:2", "s12:3",
)


def nn(a, b):
    return lax.dot_general(a, b, (((1,), (0,)), ((), ())), preferred_element_type=F32)


def nt(a, b):
    return lax.dot_general(a, b, (((1,), (1,)), ((), ())), preferred_element_type=F32)


def tn(a, b):
    return lax.dot_general(a, b, (((0,), (0,)), ((), ())), preferred_element_type=F32)


def scratch(dims):
    D, F, T, R, O = dims["D"], dims["F"], dims["T"], dims["R"], dims["O"]
    v = pltpu.VMEM
    return {
        "wg": v((D, F), BF16),
        "wu": v((D, F), BF16),
        "wd": v((F, D), BF16),
        "xa": v((2, NB, NX * NH, NC, R, D), BF16),
        "part": v((2, 3, NZ, NY, O, F), F32),
        "far_s": v((NB, 2, 2, O, F), BF16),
        "far_r": v((NB, 2, 2, O, F), BF16),
        "dir_s": v((NB, 2, 2, O, F), BF16),
        "dir_r": v((NB, 2, 2, O, F), BF16),
        "rel_s": v((NB, 2, 2, O, F), BF16),
        "rel_r": v((NB, 2, 2, O, F), BF16),
        "zsum": v((NB, NY, 2, O, F), F32),
        "gy_r": v((NB, 2, O, F), F32),
        "sy_s": v((NB, NZ, O, F), BF16),
        "sy_r": v((NB, NZ, O, F), BF16),
        "sz_s": v((NB, 3, O, F), BF16),
        "sz_r": v((NB, 3, O, F), BF16),
        "s_own": v((NB, O, F), F32),
        "hgu": v((3, NB, NZ, NY, O, F), BF16),
        "igp": v((NB, NX * NH, NC, R, D), F32),
        "co_r": v((NB, NX * NH, R, D), F32),
        "xs_s": v((NB, 3, NH, R, D), BF16),
        "xs_r": v((NB, 3, NH, R, D), BF16),
        "igx": v((NB, NH, R, D), F32),
        "h_r": v((NB, R, D), F32),
        "acc_g": v((D, F), F32),
        "acc_u": v((D, F), F32),
        "acc_d": v((F, D), F32),
        "st_g": v((D, F), BF16),
        "st_u": v((D, F), BF16),
        "st_d": v((F, D), BF16),
        "ssem": pltpu.SemaphoreType.DMA((NB * 40,)),
        "rsem": pltpu.SemaphoreType.DMA((NB * 40,)),
        "lsem": pltpu.SemaphoreType.DMA((8,)),
    }


def kernel(dims, names, x_ref, c_ref, wg_hbm, wu_hbm, wd_hbm, ig_ref, gg_hbm, ug_hbm, dg_hbm, *refs):
    D, F, T, R, O = dims["D"], dims["F"], dims["T"], dims["R"], dims["O"]
    s = dict(zip(names, refs))
    row, col = lax.axis_index("row"), lax.axis_index("col")
    yi, zi = row // NZ, row % NZ
    xi, hi, ci = col // (NH * NC), (col // NC) % NH, col % NC
    y_o, h_o, c_o = 1 - yi, 1 - hi, 1 - ci

    def zn(k):
        return (zi + k) % NZ

    def xn(k):
        return (xi + k) % NX

    def at_z(k):
        return (yi * NZ + zn(k), col)

    def at_x(k):
        return (row, xn(k) * (NH * NC) + hi * NC + ci)

    at_y = (y_o * NZ + zi, col)
    at_h = (row, xi * (NH * NC) + h_o * NC + ci)
    at_c = (row, xi * (NH * NC) + hi * NC + c_o)

    loads = [
        pltpu.make_async_copy(src, s[dst], s["lsem"].at[i])
        for i, (src, dst) in enumerate(((wg_hbm, "wg"), (wu_hbm, "wu"), (wd_hbm, "wd")))
    ]
    for load in loads:
        load.start()

    barrier = pltpu.get_barrier_semaphore()
    peers = [at_z(1), at_z(2), at_z(3), at_x(1), at_x(2), at_x(3), at_y, at_h, at_c]
    for peer in peers:
        pl.semaphore_signal(barrier, inc=1, device_id=peer, device_id_type=MESH)
    pl.semaphore_wait(barrier, len(peers))

    msgs = {}

    def send(name, b, src, dst, peer):
        i = len(msgs)
        copy = pltpu.make_async_remote_copy(
            src, dst, s["ssem"].at[i], s["rsem"].at[i], device_id=peer, device_id_type=MESH
        )
        copy.start()
        msgs[name, b] = copy

    def got(name, b):
        msgs[name, b].wait_recv()

    xa, hgu, part = s["xa"], s["hgu"], s["part"]

    def a1(b):
        xa[0, b, xi * NH + hi, ci] = x_ref[b * R : (b + 1) * R]
        xa[1, b, xi * NH + hi, ci] = c_ref[b * R : (b + 1) * R]
        mine = xa.at[:, b, xi * NH + hi, ci]
        send("a_h", b, mine, mine, at_h)
        for k in (1, 3, 2):
            send(f"a_x{k}", b, mine, mine, at_x(k))

    def a2(b):
        got("a_h", b)
        other = xa.at[:, b, xi * NH + h_o, ci]
        for k in (1, 3, 2):
            send(f"a_hx{k}", b, other, other, at_x(k))

    def a3(b):
        for k in (1, 3, 2):
            got(f"a_x{k}", b)
            got(f"a_hx{k}", b)
        same = xa.at[:, b, :, ci]
        send("a_c", b, same, same, at_c)

    def w(b):
        for load in loads:
            load.wait()

    def s1(b):
        got("a_c", b)
        p = b % 2
        x_all = xa[0, b].reshape(T, D)
        c_all = xa[1, b].reshape(T, D)
        part[p, 0] = nn(x_all, s["wg"][...]).reshape(NZ, NY, O, F)
        part[p, 1] = nn(x_all, s["wu"][...]).reshape(NZ, NY, O, F)
        for half, k in ((0, 1), (1, 3)):
            for i in range(2):
                s["far_s"][b, half, i] = part[p, i, zn(2), half].astype(BF16)
            send(f"far{half}", b, s["far_s"].at[b, half], s["far_r"].at[b, half], at_z(k))
        for way, k in ((0, 1), (1, 3)):
            for i in range(2):
                s["dir_s"][b, way, i] = part[p, i, zn(k), 1 - way].astype(BF16)
            send(f"dir{way}", b, s["dir_s"].at[b, way], s["dir_r"].at[b, way], at_z(k))
        part[p, 2] = nt(c_all, s["wd"][...]).reshape(NZ, NY, O, F)
        for z in range(NZ):
            s["sy_s"][b, z] = part[p, 2, z, y_o].astype(BF16)
        send("sy", b, s["sy_s"].at[b], s["sy_r"].at[b], at_y)

    def s2(b):
        p = b % 2
        for half, k in ((0, 1), (1, 3)):
            got(f"far{half}", b)
            for i in range(2):
                s["rel_s"][b, half, i] = (part[p, i, zn(k), half] + s["far_r"][b, half, i].astype(F32)).astype(BF16)
            send(f"rel{half}", b, s["rel_s"].at[b, half], s["rel_r"].at[b, half], at_z(k))

    def s3(b):
        p = b % 2
        got("sy", b)
        for k in (2, 1, 3):
            s["sz_s"][b, k - 1] = (part[p, 2, zn(k), yi] + s["sy_r"][b, zn(k)].astype(F32)).astype(BF16)
            send(f"sz{k}", b, s["sz_s"].at[b, k - 1], s["sz_r"].at[b, k - 1], at_z(k))
        s["s_own"][b] = part[p, 2, zi, yi] + s["sy_r"][b, zi].astype(F32)

    def s4(b):
        p = b % 2
        for half in range(2):
            got(f"dir{1 - half}", b)
            got(f"rel{half}", b)
            for i in range(2):
                s["zsum"][b, half, i] = (
                    part[p, i, zi, half]
                    + s["rel_r"][b, half, i].astype(F32)
                    + s["dir_r"][b, 1 - half, i].astype(F32)
                )
        send("gy", b, s["zsum"].at[b, y_o], s["gy_r"].at[b], at_y)

    def s5(b):
        got("gy", b)
        for k in (1, 2, 3):
            got(f"sz{k}", b)
        for j in range(0, O, 16):
            rows = slice(j, j + 16)
            gate = s["zsum"][b, yi, 0, rows] + s["gy_r"][b, 0, rows]
            up = s["zsum"][b, yi, 1, rows] + s["gy_r"][b, 1, rows]
            slope = s["s_own"][b, rows]
            for k in range(3):
                slope = slope + s["sz_r"][b, k, rows].astype(F32)
            sig = jax.nn.sigmoid(gate)
            act = gate * sig
            deriv = sig * (1.0 + gate * (1.0 - sig))
            hgu[0, b, zi, yi, rows] = (act * up).astype(BF16)
            hgu[1, b, zi, yi, rows] = (slope * up * deriv).astype(BF16)
            hgu[2, b, zi, yi, rows] = (slope * act).astype(BF16)
        mine = hgu.at[pl.ds(1, 2), b, zi, yi]
        send("c_y", b, mine, mine, at_y)
        mine = hgu.at[:, b, zi, yi]
        send("c_z1", b, mine, mine, at_z(1))
        send("c_z3", b, mine, mine, at_z(3))

    def s6a(b):
        got("c_y", b)
        other = hgu.at[pl.ds(1, 2), b, zi, y_o]
        send("c_yz1", b, other, other, at_z(1))
        send("c_yz3", b, other, other, at_z(3))

    def s6b(b):
        got("c_z1", b)
        below = hgu.at[pl.ds(1, 2), b, zn(3), yi]
        send("f_g1", b, below, below, at_z(1))
        below = hgu.at[0, b, zn(3), yi, pl.ds(0, O // 2)]
        send("f_h1", b, below, below, at_z(1))
        got("c_z3", b)
        above = hgu.at[0, b, zn(1), yi, pl.ds(O // 2, O // 2)]
        send("f_h3", b, above, above, at_z(3))

    def s6c(b):
        got("c_yz3", b)
        above = hgu.at[pl.ds(1, 2), b, zn(1), y_o]
        send("f_g3", b, above, above, at_z(3))
        got("c_yz1", b)

    def s7(b):
        got("f_h1", b)
        got("f_h3", b)
        mine = hgu.at[0, b, :, yi]
        send("h_y", b, mine, mine, at_y)

    def s8(b):
        got("f_g1", b)
        got("f_g3", b)
        gd = hgu[1, b].reshape(T, F)
        ud = hgu[2, b].reshape(T, F)
        s["igp"][b] = (nt(gd, s["wg"][...]) + nt(ud, s["wu"][...])).reshape(NX * NH, NC, R, D)
        send("co", b, s["igp"].at[b, :, c_o], s["co_r"].at[b], at_c)

    def s9(b):
        got("h_y", b)

    def s10(b):
        got("co", b)
        for k in (2, 1, 3):
            for h in range(NH):
                at = xn(k) * NH + h
                s["xs_s"][b, k - 1, h] = (s["igp"][b, at, ci] + s["co_r"][b, at]).astype(BF16)
            send(f"xs{k}", b, s["xs_s"].at[b, k - 1], s["xs_r"].at[b, k - 1], at_x(k))

    def s11(b):
        for k in (1, 3, 2):
            got(f"xs{k}", b)
        for h in range(NH):
            at = xi * NH + h
            total = s["igp"][b, at, ci] + s["co_r"][b, at]
            for k in range(3):
                total = total + s["xs_r"][b, k, h].astype(F32)
            s["igx"][b, h] = total
        send("h", b, s["igx"].at[b, h_o], s["h_r"].at[b], at_h)

    def s12(b):
        got("h", b)
        ig_ref[b * R : (b + 1) * R] = (s["igx"][b, hi] + s["h_r"][b]).astype(BF16)

    stores = []

    def g(step):
        head, tail = slice(0, NB - 1), slice(NB - 1, NB)
        n_head, n_tail = (NB - 1) * T, T
        if step == 0:
            x_h, c_h = xa[0, head].reshape(n_head, D), xa[1, head].reshape(n_head, D)
            s["acc_g"][...] = tn(x_h, hgu[1, head].reshape(n_head, F))
            s["acc_u"][...] = tn(x_h, hgu[2, head].reshape(n_head, F))
            s["acc_d"][...] = tn(hgu[0, head].reshape(n_head, F), c_h)
            return
        x_t, c_t = xa[0, tail].reshape(n_tail, D), xa[1, tail].reshape(n_tail, D)
        if step == 1:
            s["st_g"][...] = (s["acc_g"][...] + tn(x_t, hgu[1, tail].reshape(n_tail, F))).astype(BF16)
            out = (s["st_g"], gg_hbm)
        if step == 2:
            s["st_u"][...] = (s["acc_u"][...] + tn(x_t, hgu[2, tail].reshape(n_tail, F))).astype(BF16)
            out = (s["st_u"], ug_hbm)
        if step == 3:
            s["st_d"][...] = (s["acc_d"][...] + tn(hgu[0, tail].reshape(n_tail, F), c_t)).astype(BF16)
            out = (s["st_d"], dg_hbm)
        store = pltpu.make_async_copy(*out, s["lsem"].at[2 + step])
        store.start()
        stores.append(store)

    tasks = dict(a1=a1, a2=a2, a3=a3, w=w, s1=s1, s2=s2, s3=s3, s4=s4, s5=s5, s6a=s6a, s6b=s6b, s6c=s6c)
    tasks.update(s7=s7, s8=s8, s9=s9, s10=s10, s11=s11, s12=s12, g=g)
    for entry in ORDER:
        name, b = entry.split(":")
        tasks[name](int(b))

    for copy in msgs.values():
        copy.wait_send()
    for store in stores:
        store.wait()


def shards(x, c, wg, wu, wd):
    tokens, D = x.shape
    F = wg.shape[1]
    R = tokens // NB
    T = R * NX * NH * NC
    dims = {"D": D, "F": F, "T": T, "R": R, "O": T // (NZ * NY)}
    shapes = scratch(dims)
    vmem, anywhere = pl.BlockSpec(memory_space=pltpu.VMEM), pl.BlockSpec(memory_space=pl.ANY)
    names = tuple(shapes)

    def body(*refs):
        kernel(dims, names, *refs)

    return tuple(
        pl.pallas_call(
            body,
            name="swiglu_block",
            out_shape=[
                jax.ShapeDtypeStruct(x.shape, BF16),
                jax.ShapeDtypeStruct(wg.shape, BF16),
                jax.ShapeDtypeStruct(wu.shape, BF16),
                jax.ShapeDtypeStruct(wd.shape, BF16),
            ],
            in_specs=[vmem, vmem, anywhere, anywhere, anywhere],
            out_specs=[vmem, anywhere, anywhere, anywhere],
            scratch_shapes=list(shapes.values()),
            compiler_params=pltpu.CompilerParams(
                collective_id=0, has_side_effects=True, vmem_limit_bytes=62 * 2**20
            ),
            cost_estimate=pl.CostEstimate(
                flops=16 * NB * T * D * F, bytes_accessed=12 * D * F, transcendentals=0
            ),
        )(x, c, wg, wu, wd)
    )


def solution(mesh):
    placed = (P("col", "row"), P("col", "row"), P("row", "col"), P("row", "col"), P("col", "row"))
    return jax.shard_map(
        shards,
        mesh=mesh,
        in_specs=placed,
        out_specs=(P("col", "row"), P("row", "col"), P("row", "col"), P("col", "row")),
        check_vma=False,
    )
```

time: 465 us -> 127 us (0.27)
  waiting for transfers between devices: 393 us -> 0 us
  Pallas kernels: 0 us -> 117 us
  matrix products: 42.7 us -> 0 us
  between operations: 14.2 us -> 0.64 us
  other arithmetic: 7.48 us -> 0 us
    reduce_scatter x3 -> x0, waiting for transfers between devices: 203 us -> none  [the longest x1 84.6 us: shards(): lax.psum_scatter(jnp.concatenate([gate_part, up_part], axis=1), 'row', sc...]
    all_gather x5 -> x0, waiting for transfers between devices: 187 us -> none  [the longest x1 52.5 us: shards(): lax.all_gather(cotangent, 'col', axis=0, tiled=True)]
    pallas_call x0 -> x1, Pallas kernels: none -> 117 us  [shards(): pl.pallas_call(body, name='swiglu_block', out_shape=[jax.ShapeDtypeStruct...]
    dot_general x8 -> x0, matrix products: 42.7 us -> none  [the longest x3 19.8 us: dot_last(): lax.dot_general(left, right, (((1,), (1,)), ((), ())), preferred_element_...]
  transfers between devices with their start and end apart: 8 -> 0, of which waited for: 8 -> 0; matrix products, arithmetic and copies ran while one was open for 12% -> 0% of each run, Pallas kernels for 0% -> 0%
where the time goes in v1:
time: 127 us; the launch traced here: 126 us
  Pallas kernels  117 us (92%)
  local copies, waits for them, and re-layouts  7.97 us (6%)
    pallas_call x1, Pallas kernels, shards(): pl.pallas_call(body, name='swiglu_block', out_shape=[jax.ShapeDtypeStruct...  117 us
    unnamed x8, local copies, waits for them, and re-layouts  7.97 us

profile of v1, /device:TPU:0, one launch (start us, length us, event | category | flops | bytes accessed | tf_op | source)
XLA Modules:
  0.0 125.6 jit_solution(8900234097813093791)
XLA Ops:
  0.6 117.0 %swiglu_block.1 = (bf16[64,1024]{1,0:T(8,128)(2,1)}, bf16[1024,896]{1,0:T(8,128)(2,1)}, bf16[1024,896]{1,0:T(8,128)(2,1)}, bf16[896,1024]{1,0:T(8,128)(2,1)}) custom-call(bf16[64,1024]{1,0:T(8,128)(2,1)} %refs_0_.1, bf16[64,1024]{1,0:T(8,128)(2,1)} %refs_1_.1, bf16[1024,896]{1,0:T(8,128)(2,1)} %refs_2_.1, bf16[1024,896]{1,0:T(8,128)(2,1)} %refs_3_.1, ...), custom_call_target="tpu_custom_call" | custom-call | flops 15032385536 | bytes 11010048 | tf_op jit(solution)/shard_map/swiglu_block/pallas_call | solution.py:338
  117.6 1.6 %copy.13 = bf16[64,1024]{1,0:T(8,128)(2,1)} copy(bf16[64,1024]{1,0:T(8,128)(2,1)} %get-tuple-element.8) | data formatting | bytes 262144
  119.2 0.0 copy-start.1
  119.2 3.0 %copy.14 = bf16[1024,896]{1,0:T(8,128)(2,1)} copy(bf16[1024,896]{1,0:T(8,128)(2,1)} %get-tuple-element.9) | data formatting | bytes 3670016
  122.2 0.0 copy-done.1
  122.2 0.0 copy-start
  122.2 1.2 copy.15
  123.4 0.9 copy-done
  124.4 1.2 copy.16
Async XLA Ops:
  119.2 3.0 %copy-start.1 = (bf16[1024,896]{1,0:T(8,128)(2,1)S(1)}, bf16[1024,896]{1,0:T(8,128)(2,1)}, u32[]{:S(2)}) copy-start(bf16[1024,896]{1,0:T(8,128)(2,1)} %get-tuple-element.10) | copy-start | bytes 5505028
  122.2 2.2 %copy-start = (bf16[896,1024]{1,0:T(8,128)(2,1)S(1)}, bf16[896,1024]{1,0:T(8,128)(2,1)}, u32[]{:S(2)}) copy-start(bf16[896,1024]{1,0:T(8,128)(2,1)} %get-tuple-element.11) | copy-start | bytes 5505028

commit v2 on v0

v2 whole, which is shorter than its diff:
```python
import jax
import jax.numpy as jnp
from jax import lax
from jax.experimental import pallas as pl
from jax.experimental.pallas import tpu as pltpu
from jax.sharding import PartitionSpec as P

MESH = pl.DeviceIdType.MESH
F32, BF16 = jnp.float32, jnp.bfloat16
NZ, NY, NX, NH, NC = 4, 2, 4, 2, 2
STEPS = (0, 0, 1, 3, 2)
UNITS = ((0,), (1,), (2, 3), (4, 5), (6, 7))
FIRST = {1: 2, 3: 4, 2: 6}
CUT = 512

ORDER = (
    "aox:0", "axx:2", "aoc:0", "axc:3", "axx:3", "axc:2", "s1g:0", "ahx:0", "azx:2", "azx:3", "s1s:0", "s2:0",
    "ahc:0", "azc:2", "s1g:1", "azc:3", "axx:4", "acx:2", "s1s:1", "azx:4", "s3:0", "azc:4", "s4:0", "s2:1",
    "axc:4", "s1g:2", "acc:2", "acx:3", "s1s:2", "acc:3", "s2:2", "s1g:3", "s1s:3", "acx:4", "s4:2", "s3:2",
    "s2:3", "acc:4", "s1g:4", "s3b:2", "s1s:4", "s3b:0", "s4:3", "s2:4", "s3:4", "s5:2", "s4:4", "s3b:4",
    "s6a:2", "s3:3", "s5:4", "s3b:3", "s3:1", "s6a:4", "s4:1", "s6b:4", "s5:3", "s6c:4", "s5h:2", "s6a:3",
    "s5h:3", "s8:4", "s3b:1", "s6h:2", "s6b:2", "s6b:3", "s6c:2", "s10:4", "s6c:3", "s6h:3", "s5:0", "s5h:4",
    "s7:2", "s5h:0", "s5:1", "gg:3", "s5h:1", "s8:2", "s8:3", "s7:3", "gu:2", "s10:2", "s6h:4", "s9:2",
    "s10:3", "s6h:0", "s6a:0", "gg:1", "gg:2", "s6a:1", "s7:4", "s6h:1", "s6b:0", "gu:3", "s6c:0", "s9:3",
    "s7:0", "gd:1", "s6c:1", "s6b:1", "gu:1", "s8:0", "s7:1", "s8:1", "s9:4", "s10:0", "gg:0", "gd:2",
    "s10:1", "s9:0", "s11:0", "s9:1", "gd:0", "gd:3", "gu:0", "s12:0",
)


def nn(a, b):
    return lax.dot_general(a, b, (((1,), (0,)), ((), ())), preferred_element_type=F32)


def nt(a, b):
    return lax.dot_general(a, b, (((1,), (1,)), ((), ())), preferred_element_type=F32)


def tn(a, b):
    return lax.dot_general(a, b, (((0,), (0,)), ((), ())), preferred_element_type=F32)


def scratch(dims):
    D, F, R = dims["D"], dims["F"], dims["R"]
    U = NX * NH
    v = pltpu.VMEM
    shapes = {
        "wg": v((D, F), BF16),
        "wu": v((D, F), BF16),
        "wd": v((F, D), BF16),
        "xa": v((2, U, NC, R, D), BF16),
        "hgu": v((3, U * NC * R, F), BF16),
        "ig_o": v((U, R, D), F32),
        "ig_m": v((U, R, D), F32),
        "co_r": v((U, R, D), F32),
        "xs_r": v((U, R, D), F32),
        "h_s": v((R, D), BF16),
        "h_r": v((R, D), BF16),
        "acc_g": v((D, F), F32),
        "acc_u": v((D, F), F32),
        "acc_d": v((F, D), F32),
        "st_g": v((D, F), BF16),
        "st_u": v((D, F), BF16),
        "st_d": v((F, D), BF16),
        "ssem": pltpu.SemaphoreType.DMA((240,)),
        "rsem": pltpu.SemaphoreType.DMA((240,)),
        "lsem": pltpu.SemaphoreType.DMA((11,)),
    }
    for b, units in enumerate(UNITS):
        T = len(units) * NC * R
        O = T // (NZ * NY)
        if b < 4:
            shapes[f"part{b}"] = v((3, T, F), F32)
        for name in ("far_s", "far_r", "dir_s", "dir_r", "rel_s", "rel_r"):
            shapes[f"{name}{b}"] = v((2, 2, O, F), BF16)
        for name in ("gy_s", "gy_r"):
            shapes[f"{name}{b}"] = v((2, O, F), BF16)
        shapes[f"z_own{b}"] = v((2, O, F), F32)
        for name in ("sy_s", "sy_r"):
            shapes[f"{name}{b}"] = v((NZ * O, F), BF16)
        for name in ("sf_s", "sf_r", "sd_s", "sd_r", "sr_s", "sr_r"):
            shapes[f"{name}{b}"] = v((O, F), BF16)
        shapes[f"s_own{b}"] = v((O, F), F32)
    return shapes


def kernel(dims, names, x_hbm, c_hbm, wg_hbm, wu_hbm, wd_hbm, ig_ref, gg_hbm, ug_hbm, dg_hbm, *refs):
    D, F, R = dims["D"], dims["F"], dims["R"]
    s = dict(zip(names, refs))
    row, col = lax.axis_index("row"), lax.axis_index("col")
    yi, zi = row // NZ, row % NZ
    xi, hi, ci = col // (NH * NC), (col // NC) % NH, col % NC
    y_o = 1 - yi

    def zn(k):
        return (zi + k) % NZ

    def at_z(k):
        return (yi * NZ + zn(k), col)

    def at_x(k):
        return (row, ((xi + k) % NX) * (NH * NC) + hi * NC + ci)

    at_y = (y_o * NZ + zi, col)
    at_h = (row, xi * (NH * NC) + (1 - hi) * NC + ci)
    at_c = (row, xi * (NH * NC) + hi * NC + 1 - ci)
    xa, hgu = s["xa"], s["hgu"]
    low, high = pl.ds(0, CUT), pl.ds(CUT, F - CUT)

    def tokens(b):
        return len(UNITS[b]) * NC * R

    def owned(b):
        return tokens(b) // (NZ * NY)

    def start(b):
        return UNITS[b][0] * NC * R

    def rows(b, y, z, count=1):
        O = owned(b)
        return pl.ds(pl.multiple_of((y * NZ + z) * O, O), O * count)

    def all_rows(b, y, z, count=1):
        O = owned(b)
        return pl.ds(pl.multiple_of(start(b) + (y * NZ + z) * O, O), O * count)

    def part(b):
        return s[f"part{2 if b == 4 else b}"]

    loads = [
        pltpu.make_async_copy(src, dst, s["lsem"].at[i])
        for i, (src, dst) in enumerate(
            (
                (x_hbm, xa.at[0, 0, 0]),
                (c_hbm, xa.at[1, 0, 0]),
                (wg_hbm, s["wg"]),
                (wu_hbm, s["wu"]),
                (wd_hbm, s["wd"]),
            )
        )
    ]
    for load in loads:
        load.start()

    barrier = pltpu.get_barrier_semaphore()
    peers = [at_c, at_h, at_y, at_z(1), at_z(3), at_x(1), at_x(3), at_x(2)]
    for peer in peers:
        pl.semaphore_signal(barrier, inc=1, device_id=peer, device_id_type=MESH)
    pl.semaphore_wait(barrier, len(peers))

    msgs = {}

    def send(name, b, src, dst, peer):
        i = len(msgs)
        copy = pltpu.make_async_remote_copy(
            src, dst, s["ssem"].at[i], s["rsem"].at[i], device_id=peer, device_id_type=MESH
        )
        copy.start()
        msgs[name, b] = copy

    def got(name, b):
        msgs[name, b].wait_recv()

    def gather(tag, a):
        def own(b):
            loads[a].wait()
            send(f"aC{tag}", 0, xa.at[a, 0, 0], xa.at[a, 0, 1], at_c)
            send(f"ah{tag}", 0, xa.at[a, 0, 0], xa.at[a, 1, 0], at_h)

        def out(b):
            k = STEPS[b]
            send(f"ax{tag}", b, xa.at[a, 0, 0], xa.at[a, FIRST[k], 0], at_x(-k % NX))

        def across(b):
            got(f"ah{tag}", 0)
            send(f"aC{tag}", 1, xa.at[a, 1, 0], xa.at[a, 1, 1], at_c)

        def on(b):
            k = STEPS[b]
            send(f"az{tag}", b, xa.at[a, 1, 0], xa.at[a, FIRST[k] + 1, 0], at_x(-k % NX))

        def twin(b):
            got(f"ax{tag}", b)
            got(f"az{tag}", b)
            here = pl.ds(UNITS[b][0], 2)
            send(f"aC{tag}", b, xa.at[a, here, 0], xa.at[a, here, 1], at_c)

        return {f"ao{tag}": own, f"ax{tag}": out, f"ah{tag}": across, f"az{tag}": on, f"ac{tag}": twin}

    def block(ref, b):
        return ref[UNITS[b][0] : UNITS[b][-1] + 1].reshape(tokens(b), D)

    def s1g(b):
        got("aCx", b)
        if b == 0:
            loads[2].wait()
            loads[3].wait()
        p = part(b)
        x_all = block(xa.at[0], b)
        p[0] = nn(x_all, s["wg"][...])
        p[1] = nn(x_all, s["wu"][...])
        for half, k in ((0, 1), (1, 3)):
            for i in range(2):
                s[f"far_s{b}"][half, i] = p[i, rows(b, half, zn(2))].astype(BF16)
            send(f"far{half}", b, s[f"far_s{b}"].at[half], s[f"far_r{b}"].at[half], at_z(k))
        for way, k in ((0, 1), (1, 3)):
            for i in range(2):
                s[f"dir_s{b}"][way, i] = p[i, rows(b, 1 - way, zn(k))].astype(BF16)
            send(f"dir{way}", b, s[f"dir_s{b}"].at[way], s[f"dir_r{b}"].at[way], at_z(k))

    def s1s(b):
        got("aCc", b)
        if b == 0:
            loads[4].wait()
        p = part(b)
        p[2] = nt(block(xa.at[1], b), s["wd"][...])
        s[f"sy_s{b}"][...] = p[2, rows(b, y_o, 0, NZ)].astype(BF16)
        send("sy", b, s[f"sy_s{b}"], s[f"sy_r{b}"], at_y)

    def s2(b):
        for half, k in ((0, 1), (1, 3)):
            got(f"far{half}", b)
            for i in range(2):
                total = part(b)[i, rows(b, half, zn(k))] + s[f"far_r{b}"][half, i].astype(F32)
                s[f"rel_s{b}"][half, i] = total.astype(BF16)
            send(f"rel{half}", b, s[f"rel_s{b}"].at[half], s[f"rel_r{b}"].at[half], at_z(k))

    def pair(b, k, cols):
        return part(b)[2, rows(b, yi, zn(k)), cols] + s[f"sy_r{b}"][rows(b, 0, zn(k)), cols].astype(F32)

    def send_slope(name, b, cols, way, k):
        src, dst = s[f"{name}_s{b}"].at[:, cols], s[f"{name}_r{b}"].at[:, cols]
        send(f"{name}{way}", b, src, dst, at_z(k))

    def s3(b):
        got("sy", b)
        s[f"sf_s{b}"][...] = pair(b, 2, slice(None)).astype(BF16)
        send_slope("sf", b, low, 0, 1)
        send_slope("sf", b, high, 1, 3)
        s[f"sd_s{b}"][:, high] = pair(b, 1, high).astype(BF16)
        send_slope("sd", b, high, 0, 1)
        s[f"sd_s{b}"][:, low] = pair(b, 3, low).astype(BF16)
        send_slope("sd", b, low, 1, 3)
        s[f"s_own{b}"][...] = pair(b, 0, slice(None))

    def s3b(b):
        for way, k, cols in ((0, 1, low), (1, 3, high)):
            got(f"sf{way}", b)
            s[f"sr_s{b}"][:, cols] = (pair(b, k, cols) + s[f"sf_r{b}"][:, cols].astype(F32)).astype(BF16)
            send_slope("sr", b, cols, way, k)

    def s4(b):
        for half in range(2):
            got(f"dir{1 - half}", b)
            got(f"rel{half}", b)

        def total(i, y):
            here = part(b)[i, rows(b, y, zi)]
            return here + s[f"rel_r{b}"][y, i].astype(F32) + s[f"dir_r{b}"][1 - y, i].astype(F32)

        for i in range(2):
            s[f"gy_s{b}"][i] = total(i, y_o).astype(BF16)
        send("gy", b, s[f"gy_s{b}"], s[f"gy_r{b}"], at_y)
        for i in range(2):
            s[f"z_own{b}"][i] = total(i, yi)

    def s5(b):
        got("gy", b)
        for way in range(2):
            got(f"sr{way}", b)
            got(f"sd{way}", b)
        for j in range(0, owned(b), 16):
            at = slice(j, j + 16)
            gate = s[f"z_own{b}"][0, at] + s[f"gy_r{b}"][0, at].astype(F32)
            up = s[f"z_own{b}"][1, at] + s[f"gy_r{b}"][1, at].astype(F32)
            slope = s[f"s_own{b}"][at] + s[f"sr_r{b}"][at].astype(F32) + s[f"sd_r{b}"][at].astype(F32)
            sig = jax.nn.sigmoid(gate)
            act = gate * sig
            deriv = sig * (1.0 + gate * (1.0 - sig))
            to = pl.ds(pl.multiple_of(start(b) + (yi * NZ + zi) * owned(b) + j, 16), 16)
            hgu[0, to] = (act * up).astype(BF16)
            hgu[1, to] = (slope * up * deriv).astype(BF16)
            hgu[2, to] = (slope * act).astype(BF16)
        mine = hgu.at[pl.ds(1, 2), all_rows(b, yi, zi)]
        send("c_y", b, mine, mine, at_y)
        send("c_z1", b, mine, mine, at_z(1))
        send("c_z3", b, mine, mine, at_z(3))

    def s5h(b):
        mine = hgu.at[0, all_rows(b, yi, zi)]
        send("h_z1", b, mine, mine, at_z(1))
        send("h_z3", b, mine, mine, at_z(3))

    def s6a(b):
        got("c_y", b)
        other = hgu.at[pl.ds(1, 2), all_rows(b, y_o, zi)]
        send("c_yz1", b, other, other, at_z(1))
        send("c_yz3", b, other, other, at_z(3))

    def s6b(b):
        got("c_z1", b)
        below = hgu.at[pl.ds(1, 2), all_rows(b, yi, zn(3))]
        send("f_g1", b, below, below, at_z(1))
        got("c_z3", b)

    def s6c(b):
        got("c_yz3", b)
        above = hgu.at[pl.ds(1, 2), all_rows(b, y_o, zn(1))]
        send("f_g3", b, above, above, at_z(3))
        got("c_yz1", b)

    def s6h(b):
        got("h_z1", b)
        below = hgu.at[0, all_rows(b, yi, zn(3)), low]
        send("f_h1", b, below, below, at_z(1))
        got("h_z3", b)
        above = hgu.at[0, all_rows(b, yi, zn(1)), high]
        send("f_h3", b, above, above, at_z(3))

    def s7(b):
        got("f_h1", b)
        got("f_h3", b)
        mine = hgu.at[0, all_rows(b, yi, 0, NZ)]
        send("h_y", b, mine, mine, at_y)

    def s8(b):
        got("f_g1", b)
        got("f_g3", b)
        n = len(UNITS[b])
        here = pl.ds(UNITS[b][0], n)

        def of_core(core):
            at = slice(start(b), start(b) + tokens(b))
            gd = hgu[1, at].reshape(n, NC, R, F)[:, core].reshape(n * R, F)
            ud = hgu[2, at].reshape(n, NC, R, F)[:, core].reshape(n * R, F)
            return (nt(gd, s["wg"][...]) + nt(ud, s["wu"][...])).reshape(n, R, D)

        s["ig_o"][here] = of_core(1)
        send("co", b, s["ig_o"].at[here], s["co_r"].at[here], at_c)
        s["ig_m"][here] = of_core(0)

    def s9(b):
        got("h_y", b)

    def s10(b):
        got("co", b)
        here = pl.ds(UNITS[b][0], len(UNITS[b]))
        s["ig_m"][here] += s["co_r"][here]
        if b >= 2:
            k = STEPS[b]
            send("xs", b, s["ig_m"].at[here], s["xs_r"].at[pl.ds(FIRST[-k % NX], 2)], at_x(k))

    def gathered(unit):
        total = s["ig_m"][unit]
        for k in (1, 3, 2):
            total = total + s["xs_r"][FIRST[k] + unit]
        return total

    def s11(b):
        for step in (2, 3, 4):
            got("xs", step)
        s["h_s"][...] = gathered(1).astype(BF16)
        send("h", 0, s["h_s"], s["h_r"], at_h)

    def s12(b):
        mine = gathered(0)
        got("h", 0)
        ig_ref[...] = (mine + s["h_r"][...].astype(F32)).astype(BF16)

    spans = (slice(0, 2), slice(2, 4), slice(4, 6), slice(6, 8))
    stores = []

    def grad(left, right, acc, stage, out):
        seen = []

        def g(step):
            seen.append(step)
            if len(seen) == 1:
                acc[...] = tn(left(step), right(step))
            elif len(seen) < len(spans):
                acc[...] += tn(left(step), right(step))
            else:
                half = stage.shape[0] // 2
                for at in (pl.ds(0, half), pl.ds(half, half)):
                    stage[at] = (acc[at] + tn(left(step, at), right(step))).astype(BF16)
                    store = pltpu.make_async_copy(stage.at[at], out.at[at], s["lsem"].at[5 + len(stores)])
                    store.start()
                    stores.append(store)

        return g

    def activations(a):
        def pick(step, at=slice(None)):
            return xa[a, spans[step], :, :, at].reshape(-1, D if isinstance(at, slice) else at.size)

        return pick

    def results(a):
        def pick(step, at=slice(None)):
            return hgu[a, spans[step].start * NC * R : spans[step].stop * NC * R, at]

        return pick

    tasks = gather("x", 0) | gather("c", 1)
    tasks.update(s1g=s1g, s1s=s1s, s2=s2, s3=s3, s3b=s3b, s4=s4, s5=s5, s5h=s5h, s6a=s6a, s6b=s6b, s6c=s6c)
    tasks.update(s6h=s6h, s7=s7, s8=s8, s9=s9, s10=s10, s11=s11, s12=s12)
    tasks["gg"] = grad(activations(0), results(1), s["acc_g"], s["st_g"], gg_hbm)
    tasks["gu"] = grad(activations(0), results(2), s["acc_u"], s["st_u"], ug_hbm)
    tasks["gd"] = grad(results(0), activations(1), s["acc_d"], s["st_d"], dg_hbm)
    for entry in ORDER:
        name, b = entry.split(":")
        tasks[name](int(b))

    for copy in msgs.values():
        copy.wait_send()
    for store in stores:
        store.wait()


def place(*refs):
    n = 4
    src, dst, buf, (sem_in, sem_out) = refs[:n], refs[n : 2 * n], refs[2 * n : 3 * n], refs[3 * n :]
    moves = []
    for a in range(n):
        pieces = 2 if a else 1
        rows = src[a].shape[0] // pieces
        for j in range(pieces):
            at, i = pl.ds(j * rows, rows), len(moves)
            come = pltpu.make_async_copy(src[a].at[at], buf[a].at[at], sem_in.at[i])
            come.start()
            moves.append((come, pltpu.make_async_copy(buf[a].at[at], dst[a].at[at], sem_out.at[i])))
    for come, go in moves:
        come.wait()
        go.start()
    for _, go in moves:
        go.wait()


def shards(x, c, wg, wu, wd):
    R, D = x.shape
    F = wg.shape[1]
    dims = {"D": D, "F": F, "R": R}
    shapes = scratch(dims)
    vmem, anywhere = pl.BlockSpec(memory_space=pltpu.VMEM), pl.BlockSpec(memory_space=pl.ANY)
    names = tuple(shapes)

    def body(*refs):
        kernel(dims, names, *refs)

    out_shape = [jax.ShapeDtypeStruct(a.shape, BF16) for a in (x, wg, wu, wd)]
    outs = pl.pallas_call(
        body,
        name="swiglu_block",
        out_shape=out_shape,
        in_specs=[anywhere] * 5,
        out_specs=[vmem, anywhere, anywhere, anywhere],
        scratch_shapes=list(shapes.values()),
        compiler_params=pltpu.CompilerParams(collective_id=0, has_side_effects=True, vmem_limit_bytes=62 * 2**20),
        cost_estimate=pl.CostEstimate(flops=16 * NX * NH * NC * R * D * F, bytes_accessed=12 * D * F, transcendentals=0),
    )(x, c, wg, wu, wd)
    return tuple(
        pl.pallas_call(
            place,
            name="place_outputs",
            out_shape=out_shape,
            in_specs=[anywhere] * 4,
            out_specs=[anywhere] * 4,
            scratch_shapes=[pltpu.VMEM(a.shape, BF16) for a in out_shape] + [pltpu.SemaphoreType.DMA((8,))] * 2,
            compiler_params=pltpu.CompilerParams(vmem_limit_bytes=62 * 2**20),
            cost_estimate=pl.CostEstimate(flops=0, bytes_accessed=12 * D * F, transcendentals=0),
        )(*outs)
    )


def solution(mesh):
    placed = (P("col", "row"), P("col", "row"), P("row", "col"), P("row", "col"), P("col", "row"))
    return jax.shard_map(
        shards,
        mesh=mesh,
        in_specs=placed,
        out_specs=(P("col", "row"), P("row", "col"), P("row", "col"), P("col", "row")),
        check_vma=False,
    )
```

time: 465 us -> 113 us (0.24)
  waiting for transfers between devices: 393 us -> 0 us
  Pallas kernels: 0 us -> 113 us
  matrix products: 42.7 us -> 0 us
  between operations: 14.2 us -> 0.8 us
  local copies, waits for them, and re-layouts: 7.61 us -> 0 us
  other arithmetic: 7.48 us -> 0 us
    reduce_scatter x3 -> x0, waiting for transfers between devices: 203 us -> none  [the longest x1 84.6 us: shards(): lax.psum_scatter(jnp.concatenate([gate_part, up_part], axis=1), 'row', sc...]
    all_gather x5 -> x0, waiting for transfers between devices: 187 us -> none  [the longest x1 52.5 us: shards(): lax.all_gather(cotangent, 'col', axis=0, tiled=True)]
    pallas_call x0 -> x2, Pallas kernels: none -> 113 us  [the longest x1 108 us: shards(): pl.pallas_call(body, name='swiglu_block', out_shape=out_shape, in_specs=[...]
    dot_general x8 -> x0, matrix products: 42.7 us -> none  [the longest x3 19.8 us: dot_last(): lax.dot_general(left, right, (((1,), (1,)), ((), ())), preferred_element_...]
    unnamed x8 -> x0, local copies, waits for them, and re-layouts: 7.61 us -> none
  transfers between devices with their start and end apart: 8 -> 0, of which waited for: 8 -> 0; matrix products, arithmetic and copies ran while one was open for 12% -> 0% of each run, Pallas kernels for 0% -> 0%
where the time goes in v2:
time: 113 us
  Pallas kernels  113 us (100%)
    pallas_call x1, Pallas kernels, shards(): pl.pallas_call(body, name='swiglu_block', out_shape=out_shape, in_specs=[...  108 us
    pallas_call x1, Pallas kernels, shards(): pl.pallas_call(place, name='place_outputs', out_shape=out_shape, in_specs...  4.96 us

profile of v2, /device:TPU:0, one launch (start us, length us, event | category | flops | bytes accessed | tf_op | source)
XLA Modules:
  0.0 113.4 jit_solution(632163385100780346)
XLA Ops:
  0.6 107.6 %swiglu_block.1 = (bf16[64,1024]{1,0:T(8,128)(2,1)}, bf16[1024,896]{1,0:T(8,128)(2,1)}, bf16[1024,896]{1,0:T(8,128)(2,1)}, bf16[896,1024]{1,0:T(8,128)(2,1)}) custom-call(bf16[64,1024]{1,0:T(8,128)(2,1)} %refs_0_.1, bf16[64,1024]{1,0:T(8,128)(2,1)} %refs_1_.1, bf16[1024,896]{1,0:T(8,128)(2,1)} %refs_2_.1, bf16[1024,896]{1,0:T(8,128)(2,1)} %refs_3_.1, ...), custom_call_target="tpu_custom_call" | custom-call | flops 15032385536 | bytes 11010048 | tf_op jit(solution)/shard_map/swiglu_block/pallas_call | solution.py:450
  108.3 5.0 %place_outputs.1 = (bf16[64,1024]{1,0:T(8,128)(2,1)}, bf16[1024,896]{1,0:T(8,128)(2,1)}, bf16[1024,896]{1,0:T(8,128)(2,1)}, bf16[896,1024]{1,0:T(8,128)(2,1)}) custom-call(bf16[64,1024]{1,0:T(8,128)(2,1)} %get-tuple-element.8.refs_0_, bf16[1024,896]{1,0:T(8,128)(2,1)} %get-tuple-element.9.refs_1_, bf16[1024,896]{1,0:T(8,128)(2,1)} %get-tuple-element.10.refs_2_, ...), custom_call_target="tpu_custom_call" | custom-call | bytes 11010048 | tf_op jit(solution)/shard_map/place_outputs/pallas_call | solution.py:461

commit v3 on v2

v3 whole, which is shorter than its diff:
```python
import jax
import jax.numpy as jnp
from jax import lax
from jax.experimental import pallas as pl
from jax.experimental.pallas import tpu as pltpu
from jax.sharding import PartitionSpec as P

MESH = pl.DeviceIdType.MESH
F32, BF16 = jnp.float32, jnp.bfloat16
NZ, NY, NX, NH, NC = 4, 2, 4, 2, 2
PLACE = ((0, 0), (0, 1), (1, 0), (3, 0), (1, 1), (3, 1), (2, 0), (2, 1))
UNITS = ((0,), (1,), (2, 3), (4, 5), (6, 7))
SPANS = ((0, 2), (2, 4), (4, 6), (6, 8))
HIDDEN_Y_FIRST = (0, 1, 4)
CUT = 512
ORDER = (
    0, 13, 12, 40, 52, 53, 80, 90, 16, 20, 32, 14, 15, 17, 100, 81, 72, 60, 54, 82, 55, 130, 56, 91, 57, 92,
    33, 102, 83, 73, 34, 132, 93, 112, 84, 74, 103, 122, 94, 104, 113, 142, 114, 152, 134, 133, 124, 110, 162,
    123, 144, 154, 172, 182, 143, 164, 174, 153, 192, 252, 184, 120, 101, 301, 291, 111, 202, 163, 262, 194,
    254, 131, 140, 121, 150, 264, 212, 303, 173, 183, 203, 141, 151, 160, 293, 222, 161, 193, 253, 213, 170,
    171, 200, 292, 180, 263, 181, 201, 210, 242, 204, 223, 302, 190, 250, 191, 211, 251, 214, 221, 290, 260,
    230, 220, 261, 270, 224, 231, 311, 234, 300, 243, 312, 241, 240, 310, 244, 313, 280,
)


def nn(a, b):
    return lax.dot_general(a, b, (((1,), (0,)), ((), ())), preferred_element_type=F32)


def nt(a, b):
    return lax.dot_general(a, b, (((1,), (1,)), ((), ())), preferred_element_type=F32)


def tn(a, b):
    return lax.dot_general(a, b, (((0,), (0,)), ((), ())), preferred_element_type=F32)


def scratch(dims):
    D, F, R = dims["D"], dims["F"], dims["R"]
    U = NX * NH
    v = pltpu.VMEM
    shapes = {
        "wg": v((D, F), BF16),
        "wu": v((D, F), BF16),
        "wd": v((F, D), BF16),
        "xa": v((2, U, NC, R, D), BF16),
        "hgu": v((3, U * NC * R, F), BF16),
        "ig_o": v((U, R, D), F32),
        "ig_m": v((U, R, D), F32),
        "co_r": v((U, R, D), F32),
        "xs_r": v((U, R, D), F32),
        "h_s": v((R, D), BF16),
        "h_r": v((R, D), BF16),
        "acc_g": v((D, F), F32),
        "acc_u": v((D, F), F32),
        "acc_d": v((F, D), F32),
        "st_g": v((D, F), BF16),
        "st_u": v((D, F), BF16),
        "st_d": v((F, D), BF16),
        "ssem": pltpu.SemaphoreType.DMA((240,)),
        "rsem": pltpu.SemaphoreType.DMA((240,)),
        "lsem": pltpu.SemaphoreType.DMA((11,)),
    }
    for b, units in enumerate(UNITS):
        T = len(units) * NC * R
        O = T // (NZ * NY)
        if b < 4:
            shapes["part", b] = v((3, T, F), F32)
        for name in ("far", "dir", "rel"):
            shapes[name, 0, b] = shapes[name, 1, b] = v((2, 2, O, F), BF16)
        shapes["ry", 0, b] = shapes["ry", 1, b] = v((2, O, F), BF16)
        shapes["sy", 0, b] = shapes["sy", 1, b] = v((NZ * O, F), BF16)
        for name in ("sf", "sd", "sr"):
            shapes[name, 0, b] = shapes[name, 1, b] = v((O, F), BF16)
        shapes["z_own", b] = v((2, O, F), F32)
        shapes["s_own", b] = v((O, F), F32)
    return shapes


def kernel(dims, names, x_hbm, c_hbm, wg_hbm, wu_hbm, wd_hbm, ig_ref, gg_hbm, ug_hbm, dg_hbm, *refs):
    D, F, R = dims["D"], dims["F"], dims["R"]
    s = dict(zip(names, refs))
    row, col = lax.axis_index("row"), lax.axis_index("col")
    yi, zi = row // NZ, row % NZ
    xi, hi, ci = col // (NH * NC), (col // NC) % NH, col % NC
    y_o = 1 - yi

    def zn(k):
        return (zi + k) % NZ

    def at_z(k):
        return (yi * NZ + zn(k), col)

    def at_x(k):
        return (row, ((xi + k) % NX) * (NH * NC) + hi * NC + ci)

    at_y = (y_o * NZ + zi, col)
    at_h = (row, xi * (NH * NC) + (1 - hi) * NC + ci)
    at_c = (row, xi * (NH * NC) + hi * NC + 1 - ci)
    xa, hgu = s["xa"], s["hgu"]
    low, high = pl.ds(0, CUT), pl.ds(CUT, F - CUT)
    ways = ((0, 1), (1, 3))

    def back(u):
        k, h = PLACE[u]
        return PLACE.index((-k % NX, h)), k

    def tokens(b):
        return len(UNITS[b]) * NC * R

    def owned(b):
        return tokens(b) // (NZ * NY)

    def start(b):
        return UNITS[b][0] * NC * R

    def rows(b, y, z, count=1):
        O = owned(b)
        return pl.ds(pl.multiple_of((y * NZ + z) * O, O), O * count)

    def all_rows(b, y, z, count=1):
        O = owned(b)
        return pl.ds(pl.multiple_of(start(b) + (y * NZ + z) * O, O), O * count)

    def part(b):
        return s["part", b if b < 4 else b - 2]

    loads = [
        pltpu.make_async_copy(src, dst, s["lsem"].at[i])
        for i, (src, dst) in enumerate(
            (
                (x_hbm, xa.at[0, 0, 0]),
                (c_hbm, xa.at[1, 0, 0]),
                (wg_hbm, s["wg"]),
                (wu_hbm, s["wu"]),
                (wd_hbm, s["wd"]),
            )
        )
    ]
    for load in loads:
        load.start()

    barrier = pltpu.get_barrier_semaphore()
    peers = [at_c, at_h, at_y, at_z(1), at_z(3), at_x(1), at_x(3), at_x(2)]
    for peer in peers:
        pl.semaphore_signal(barrier, inc=1, device_id=peer, device_id_type=MESH)
    pl.semaphore_wait(barrier, len(peers))

    msgs = {}

    def send(key, src, dst, peer):
        i = len(msgs)
        copy = pltpu.make_async_remote_copy(
            src, dst, s["ssem"].at[i], s["rsem"].at[i], device_id=peer, device_id_type=MESH
        )
        copy.start()
        msgs[key] = copy

    def got(*key):
        msgs[key].wait_recv()

    def gather(a):
        def own(b):
            loads[a].wait()
            send(("aC", a, 0), xa.at[a, 0, 0], xa.at[a, 0, 1], at_c)
            send(("ah", a), xa.at[a, 0, 0], xa.at[a, 1, 0], at_h)

        def along(u):
            there, k = back(u)
            src = xa.at[a, PLACE[u][1], 0]
            send(("ax", a, there), src, xa.at[a, there, 0], at_x(k))

        def across(b):
            got("ah", a)
            send(("aC", a, 1), xa.at[a, 1, 0], xa.at[a, 1, 1], at_c)

        def twin(b):
            for u in UNITS[b]:
                got("ax", a, u)
            here = pl.ds(UNITS[b][0], len(UNITS[b]))
            send(("aC", a, b), xa.at[a, here, 0], xa.at[a, here, 1], at_c)

        return [own, along, across, twin]

    def block(a, b):
        return xa[a, UNITS[b][0] : UNITS[b][-1] + 1].reshape(tokens(b), D)

    def send_z(name, b, way, k, dims=()):
        at = dims or (way,)
        send((name, way, b), s[name, 0, b].at[at], s[name, 1, b].at[at], at_z(k))

    def s1g(b):
        got("aC", 0, b)
        if b == 0:
            loads[2].wait()
            loads[3].wait()
        p = part(b)
        x_all = block(0, b)
        p[0] = nn(x_all, s["wg"][...])
        p[1] = nn(x_all, s["wu"][...])
        for half, k in ways:
            for i in range(2):
                s["far", 0, b][half, i] = p[i, rows(b, half, zn(2))].astype(BF16)
            send_z("far", b, half, k)
        for way, k in ways:
            for i in range(2):
                s["dir", 0, b][way, i] = p[i, rows(b, 1 - way, zn(k))].astype(BF16)
            send_z("dir", b, way, k)

    def s1s(b):
        got("aC", 1, b)
        if b == 0:
            loads[4].wait()
        p = part(b)
        p[2] = nt(block(1, b), s["wd"][...])
        s["sy", 0, b][...] = p[2, rows(b, y_o, 0, NZ)].astype(BF16)
        send(("sy", b), s["sy", 0, b], s["sy", 1, b], at_y)

    def s2(b):
        for half, k in ways:
            got("far", half, b)
            for i in range(2):
                total = part(b)[i, rows(b, half, zn(k))] + s["far", 1, b][half, i].astype(F32)
                s["rel", 0, b][half, i] = total.astype(BF16)
            send_z("rel", b, half, k)

    def pair(b, k, cols):
        return part(b)[2, rows(b, yi, zn(k)), cols] + s["sy", 1, b][rows(b, 0, zn(k)), cols].astype(F32)

    every = slice(None)

    def s3(b):
        got("sy", b)
        s["sf", 0, b][...] = pair(b, 2, every).astype(BF16)
        send_z("sf", b, 0, 1, (every, low))
        send_z("sf", b, 1, 3, (every, high))
        s["sd", 0, b][:, high] = pair(b, 1, high).astype(BF16)
        send_z("sd", b, 0, 1, (every, high))
        s["sd", 0, b][:, low] = pair(b, 3, low).astype(BF16)
        send_z("sd", b, 1, 3, (every, low))
        s["s_own", b][...] = pair(b, 0, every)

    def s3b(b):
        for way, k, cols in ((0, 1, low), (1, 3, high)):
            got("sf", way, b)
            s["sr", 0, b][:, cols] = (pair(b, k, cols) + s["sf", 1, b][:, cols].astype(F32)).astype(BF16)
            send_z("sr", b, way, k, (every, cols))

    def s4(b):
        for half in range(2):
            got("dir", 1 - half, b)
            got("rel", half, b)

        def total(i, y):
            here = part(b)[i, rows(b, y, zi)]
            return here + s["rel", 1, b][y, i].astype(F32) + s["dir", 1, b][1 - y, i].astype(F32)

        for i in range(2):
            s["ry", 0, b][i] = total(i, y_o).astype(BF16)
        send(("ry", b), s["ry", 0, b], s["ry", 1, b], at_y)
        for i in range(2):
            s["z_own", b][i] = total(i, yi)

    def s5(b):
        got("ry", b)
        for way in range(2):
            got("sr", way, b)
            got("sd", way, b)
        for j in range(0, owned(b), 16):
            at = slice(j, j + 16)
            gate = s["z_own", b][0, at] + s["ry", 1, b][0, at].astype(F32)
            up = s["z_own", b][1, at] + s["ry", 1, b][1, at].astype(F32)
            slope = s["s_own", b][at] + s["sr", 1, b][at].astype(F32) + s["sd", 1, b][at].astype(F32)
            sig = jax.nn.sigmoid(gate)
            act = gate * sig
            deriv = sig * (1.0 + gate * (1.0 - sig))
            to = pl.ds(pl.multiple_of(start(b) + (yi * NZ + zi) * owned(b) + j, 16), 16)
            hgu[0, to] = (act * up).astype(BF16)
            hgu[1, to] = (slope * up * deriv).astype(BF16)
            hgu[2, to] = (slope * act).astype(BF16)

    def spread(first, count, y_first):
        arrays = pl.ds(first, count)

        def put(name, way, b, at, peer):
            here = hgu.at[(arrays,) + at]
            send((name, way, b, first), here, here, peer)

        def begin(b):
            mine = (all_rows(b, yi, zi),)
            if b in y_first:
                put("cy", 0, b, mine, at_y)
            for way, k in ways:
                put("cz", way, b, mine, at_z(k))

        def second(b):
            if b in y_first:
                got("cy", 0, b, first)
                for way, k in ways:
                    put("cu", way, b, (all_rows(b, y_o, zi),), at_z(k))
            else:
                for way, k, cols in ((0, 1, low), (1, 3, high)):
                    got("cz", way, b, first)
                    put("cf", way, b, (all_rows(b, yi, zn(-k % NZ)), cols), at_z(k))

        def third(b):
            if b in y_first:
                got("cz", 0, b, first)
                put("cf", 0, b, (all_rows(b, yi, zn(3)),), at_z(1))
                got("cz", 1, b, first)
            else:
                got("cf", 0, b, first)
                got("cf", 1, b, first)
                put("cy", 0, b, (all_rows(b, yi, 0, NZ),), at_y)

        def fourth(b):
            got("cu", 1, b, first)
            put("cf", 1, b, (all_rows(b, y_o, zn(1)),), at_z(3))
            got("cu", 0, b, first)

        def last(b):
            if b in y_first:
                got("cf", 0, b, first)
                got("cf", 1, b, first)
            else:
                got("cy", 0, b, first)

        return [begin, second, third, fourth, last]

    def s8(b):
        n = len(UNITS[b])
        here = pl.ds(UNITS[b][0], n)

        def of_core(core):
            at = slice(start(b), start(b) + tokens(b))
            gd = hgu[1, at].reshape(n, NC, R, F)[:, core].reshape(n * R, F)
            ud = hgu[2, at].reshape(n, NC, R, F)[:, core].reshape(n * R, F)
            return (nt(gd, s["wg"][...]) + nt(ud, s["wu"][...])).reshape(n, R, D)

        s["ig_o"][here] = of_core(1)
        send(("co", b), s["ig_o"].at[here], s["co_r"].at[here], at_c)
        s["ig_m"][here] = of_core(0)

    def s10(b):
        got("co", b)
        here = pl.ds(UNITS[b][0], len(UNITS[b]))
        s["ig_m"][here] += s["co_r"][here]
        if b >= 2:
            for u in UNITS[b]:
                there, k = back(u)
                send(("xs", there), s["ig_m"].at[u], s["xs_r"].at[there], at_x(k))

    def gathered(h):
        total = s["ig_m"][h]
        for u, (k, other) in enumerate(PLACE):
            if k and other == h:
                total = total + s["xs_r"][u]
        return total

    def s11(b):
        for u in range(2, len(PLACE)):
            got("xs", u)
        s["h_s"][...] = gathered(1).astype(BF16)
        send(("h",), s["h_s"], s["h_r"], at_h)

    def s12(b):
        mine = gathered(0)
        got("h")
        ig_ref[...] = (mine + s["h_r"][...].astype(F32)).astype(BF16)

    stores = []

    def grad(left, right, acc, stage, out):
        seen = []

        def g(step):
            seen.append(step)
            if len(seen) == 1:
                acc[...] = tn(left(step), right(step))
            elif len(seen) < len(SPANS):
                acc[...] += tn(left(step), right(step))
            else:
                half = stage.shape[0] // 2
                for at in (pl.ds(0, half), pl.ds(half, half)):
                    stage[at] = (acc[at] + tn(left(step, at), right(step))).astype(BF16)
                    store = pltpu.make_async_copy(stage.at[at], out.at[at], s["lsem"].at[5 + len(stores)])
                    store.start()
                    stores.append(store)

        return g

    def activations(a):
        def pick(step, at=pl.ds(0, D)):
            first, end = SPANS[step]
            return xa[a, first:end, :, :, at].reshape(-1, at.size)

        return pick

    def results(a):
        def pick(step, at=pl.ds(0, F)):
            first, end = SPANS[step]
            return hgu[a, first * NC * R : end * NC * R, at]

        return pick

    tasks = [*gather(0), *gather(1), s1g, s1s, s2, s3, s3b, s4, s5]
    tasks += [*spread(1, 2, range(len(UNITS))), *spread(0, 1, HIDDEN_Y_FIRST), s8, s10, s11, s12]
    tasks.append(grad(activations(0), results(1), s["acc_g"], s["st_g"], gg_hbm))
    tasks.append(grad(activations(0), results(2), s["acc_u"], s["st_u"], ug_hbm))
    tasks.append(grad(results(0), activations(1), s["acc_d"], s["st_d"], dg_hbm))
    for entry in ORDER:
        tasks[entry // 10](entry % 10)

    for copy in msgs.values():
        copy.wait_send()
    for store in stores:
        store.wait()


def place(*refs):
    n = 4
    src, dst, buf, (sem_in, sem_out) = refs[:n], refs[n : 2 * n], refs[2 * n : 3 * n], refs[3 * n :]
    moves = []
    for a in range(n):
        pieces = 2 if a else 1
        rows = src[a].shape[0] // pieces
        for j in range(pieces):
            at, i = pl.ds(j * rows, rows), len(moves)
            come = pltpu.make_async_copy(src[a].at[at], buf[a].at[at], sem_in.at[i])
            come.start()
            moves.append((come, pltpu.make_async_copy(buf[a].at[at], dst[a].at[at], sem_out.at[i])))
    for come, go in moves:
        come.wait()
        go.start()
    for _, go in moves:
        go.wait()


def shards(x, c, wg, wu, wd):
    R, D = x.shape
    F = wg.shape[1]
    dims = {"D": D, "F": F, "R": R}
    shapes = scratch(dims)
    vmem, anywhere = pl.BlockSpec(memory_space=pltpu.VMEM), pl.BlockSpec(memory_space=pl.ANY)
    names = tuple(shapes)

    def body(*refs):
        kernel(dims, names, *refs)

    out_shape = [jax.ShapeDtypeStruct(a.shape, BF16) for a in (x, wg, wu, wd)]
    outs = pl.pallas_call(
        body,
        name="swiglu_block",
        out_shape=out_shape,
        in_specs=[anywhere] * 5,
        out_specs=[vmem, anywhere, anywhere, anywhere],
        scratch_shapes=list(shapes.values()),
        compiler_params=pltpu.CompilerParams(collective_id=0, has_side_effects=True, vmem_limit_bytes=62 * 2**20),
        cost_estimate=pl.CostEstimate(flops=16 * NX * NH * NC * R * D * F, bytes_accessed=12 * D * F, transcendentals=0),
    )(x, c, wg, wu, wd)
    return tuple(
        pl.pallas_call(
            place,
            name="place_outputs",
            out_shape=out_shape,
            in_specs=[anywhere] * 4,
            out_specs=[anywhere] * 4,
            scratch_shapes=[pltpu.VMEM(a.shape, BF16) for a in out_shape] + [pltpu.SemaphoreType.DMA((8,))] * 2,
            compiler_params=pltpu.CompilerParams(vmem_limit_bytes=62 * 2**20),
            cost_estimate=pl.CostEstimate(flops=0, bytes_accessed=12 * D * F, transcendentals=0),
        )(*outs)
    )


def solution(mesh):
    placed = (P("col", "row"), P("col", "row"), P("row", "col"), P("row", "col"), P("col", "row"))
    return jax.shard_map(
        shards,
        mesh=mesh,
        in_specs=placed,
        out_specs=(P("col", "row"), P("row", "col"), P("row", "col"), P("col", "row")),
        check_vma=False,
    )
```

time: 113 us -> 111 us (0.982)
  Pallas kernels: 113 us -> 110 us
    pallas_call x1, Pallas kernels: 108 us -> 105 us  [shards(): pl.pallas_call(body, name='swiglu_block', out_shape=out_shape, in_specs=[...]
where the time goes in v3:
time: 111 us; the launch traced here: 110 us
  Pallas kernels  110 us (99%)
    pallas_call x1, Pallas kernels, shards(): pl.pallas_call(body, name='swiglu_block', out_shape=out_shape, in_specs=[...  105 us
    pallas_call x1, Pallas kernels, shards(): pl.pallas_call(place, name='place_outputs', out_shape=out_shape, in_specs...  4.96 us

profile of v3, /device:TPU:0, one launch (start us, length us, event | category | flops | bytes accessed | tf_op | source)
XLA Modules:
  0.0 110.5 jit_solution(12732988045683823663)
XLA Ops:
  0.6 104.7 %swiglu_block.1 = (bf16[64,1024]{1,0:T(8,128)(2,1)}, bf16[1024,896]{1,0:T(8,128)(2,1)}, bf16[1024,896]{1,0:T(8,128)(2,1)}, bf16[896,1024]{1,0:T(8,128)(2,1)}) custom-call(bf16[64,1024]{1,0:T(8,128)(2,1)} %refs_0_.1, bf16[64,1024]{1,0:T(8,128)(2,1)} %refs_1_.1, bf16[1024,896]{1,0:T(8,128)(2,1)} %refs_2_.1, bf16[1024,896]{1,0:T(8,128)(2,1)} %refs_3_.1, ...), custom_call_target="tpu_custom_call" | custom-call | flops 15032385536 | bytes 11010048 | tf_op jit(solution)/shard_map/swiglu_block/pallas_call | solution.py:451
  105.4 5.0 %place_outputs.1 = (bf16[64,1024]{1,0:T(8,128)(2,1)}, bf16[1024,896]{1,0:T(8,128)(2,1)}, bf16[1024,896]{1,0:T(8,128)(2,1)}, bf16[896,1024]{1,0:T(8,128)(2,1)}) custom-call(bf16[64,1024]{1,0:T(8,128)(2,1)} %get-tuple-element.8.refs_0_, bf16[1024,896]{1,0:T(8,128)(2,1)} %get-tuple-element.9.refs_1_, bf16[1024,896]{1,0:T(8,128)(2,1)} %get-tuple-element.10.refs_2_, ...), custom_call_target="tpu_custom_call" | custom-call | bytes 11010048 | tf_op jit(solution)/shard_map/place_outputs/pallas_call | solution.py:462

commit v4 on v3

--- a/solution.py
+++ b/solution.py
@@ -12,7 +12,9 @@
 UNITS = ((0,), (1,), (2, 3), (4, 5), (6, 7))
 SPANS = ((0, 2), (2, 4), (4, 6), (6, 8))
 HIDDEN_Y_FIRST = (0, 1, 4)
+DELTAS_Y_FIRST = (0, 1, 2, 3, 4)
 CUT = 512
+IN_FLIGHT = 36
 ORDER = (
     0, 13, 12, 40, 52, 53, 80, 90, 16, 20, 32, 14, 15, 17, 100, 81, 72, 60, 54, 82, 55, 130, 56, 91, 57, 92,
     33, 102, 83, 73, 34, 132, 93, 112, 84, 74, 103, 122, 94, 104, 113, 142, 114, 152, 134, 133, 124, 110, 162,
@@ -54,12 +56,9 @@
         "acc_g": v((D, F), F32),
         "acc_u": v((D, F), F32),
         "acc_d": v((F, D), F32),
-        "st_g": v((D, F), BF16),
-        "st_u": v((D, F), BF16),
-        "st_d": v((F, D), BF16),
         "ssem": pltpu.SemaphoreType.DMA((240,)),
         "rsem": pltpu.SemaphoreType.DMA((240,)),
-        "lsem": pltpu.SemaphoreType.DMA((11,)),
+        "lsem": pltpu.SemaphoreType.DMA((5,)),
     }
     for b, units in enumerate(UNITS):
         T = len(units) * NC * R
@@ -77,7 +76,7 @@
     return shapes
 
 
-def kernel(dims, names, x_hbm, c_hbm, wg_hbm, wu_hbm, wd_hbm, ig_ref, gg_hbm, ug_hbm, dg_hbm, *refs):
+def kernel(dims, names, x_hbm, c_hbm, wg_hbm, wu_hbm, wd_hbm, ig_ref, gg_ref, ug_ref, dg_ref, *refs):
     D, F, R = dims["D"], dims["F"], dims["R"]
     s = dict(zip(names, refs))
     row, col = lax.axis_index("row"), lax.axis_index("col")
@@ -146,7 +145,7 @@
         pl.semaphore_signal(barrier, inc=1, device_id=peer, device_id_type=MESH)
     pl.semaphore_wait(barrier, len(peers))
 
-    msgs = {}
+    msgs, leaving = {}, []
 
     def send(key, src, dst, peer):
         i = len(msgs)
@@ -155,6 +154,7 @@
         )
         copy.start()
         msgs[key] = copy
+        leaving.append(copy)
 
     def got(*key):
         msgs[key].wait_recv()
@@ -368,9 +368,7 @@
         got("h")
         ig_ref[...] = (mine + s["h_r"][...].astype(F32)).astype(BF16)
 
-    stores = []
-
-    def grad(left, right, acc, stage, out):
+    def grad(left, right, acc, out):
         seen = []
 
         def g(step):
@@ -380,60 +378,45 @@
             elif len(seen) < len(SPANS):
                 acc[...] += tn(left(step), right(step))
             else:
-                half = stage.shape[0] // 2
-                for at in (pl.ds(0, half), pl.ds(half, half)):
-                    stage[at] = (acc[at] + tn(left(step, at), right(step))).astype(BF16)
-                    store = pltpu.make_async_copy(stage.at[at], out.at[at], s["lsem"].at[5 + len(stores)])
-                    store.start()
-                    stores.append(store)
+                out[...] = (acc[...] + tn(left(step), right(step))).astype(BF16)
 
         return g
 
     def activations(a):
-        def pick(step, at=pl.ds(0, D)):
+        def pick(step):
             first, end = SPANS[step]
-            return xa[a, first:end, :, :, at].reshape(-1, at.size)
+            return xa[a, first:end].reshape(-1, D)
 
         return pick
 
     def results(a):
-        def pick(step, at=pl.ds(0, F)):
+        def pick(step):
             first, end = SPANS[step]
-            return hgu[a, first * NC * R : end * NC * R, at]
+            return hgu[a, first * NC * R : end * NC * R]
 
         return pick
 
     tasks = [*gather(0), *gather(1), s1g, s1s, s2, s3, s3b, s4, s5]
-    tasks += [*spread(1, 2, range(len(UNITS))), *spread(0, 1, HIDDEN_Y_FIRST), s8, s10, s11, s12]
-    tasks.append(grad(activations(0), results(1), s["acc_g"], s["st_g"], gg_hbm))
-    tasks.append(grad(activations(0), results(2), s["acc_u"], s["st_u"], ug_hbm))
-    tasks.append(grad(results(0), activations(1), s["acc_d"], s["st_d"], dg_hbm))
+    tasks += [*spread(1, 2, DELTAS_Y_FIRST), *spread(0, 1, HIDDEN_Y_FIRST), s8, s10, s11, s12]
+    tasks.append(grad(activations(0), results(1), s["acc_g"], gg_ref))
+    tasks.append(grad(activations(0), results(2), s["acc_u"], ug_ref))
+    tasks.append(grad(results(0), activations(1), s["acc_d"], dg_ref))
     for entry in ORDER:
         tasks[entry // 10](entry % 10)
-
-    for copy in msgs.values():
+        while len(leaving) > IN_FLIGHT:
+            leaving.pop(0).wait_send()
+
+    for copy in leaving:
         copy.wait_send()
-    for store in stores:
-        store.wait()
 
 
 def place(*refs):
     n = 4
-    src, dst, buf, (sem_in, sem_out) = refs[:n], refs[n : 2 * n], refs[2 * n : 3 * n], refs[3 * n :]
-    moves = []
-    for a in range(n):
-        pieces = 2 if a else 1
-        rows = src[a].shape[0] // pieces
-        for j in range(pieces):
-            at, i = pl.ds(j * rows, rows), len(moves)
-            come = pltpu.make_async_copy(src[a].at[at], buf[a].at[at], sem_in.at[i])
-            come.start()
-            moves.append((come, pltpu.make_async_copy(buf[a].at[at], dst[a].at[at], sem_out.at[i])))
-    for come, go in moves:
-        come.wait()
-        go.start()
-    for _, go in moves:
-        go.wait()
+    moves = [pltpu.make_async_copy(refs[a], refs[n + a], refs[2 * n].at[a]) for a in range(n)]
+    for move in moves:
+        move.start()
+    for move in moves:
+        move.wait()
 
 
 def shards(x, c, wg, wu, wd):
@@ -451,24 +434,24 @@
     outs = pl.pallas_call(
         body,
         name="swiglu_block",
-        out_shape=out_shape,
+        out_shape=[pltpu.VMEM(a.shape, BF16) for a in out_shape],
         in_specs=[anywhere] * 5,
-        out_specs=[vmem, anywhere, anywhere, anywhere],
+        out_specs=[vmem] * 4,
         scratch_shapes=list(shapes.values()),
-        compiler_params=pltpu.CompilerParams(collective_id=0, has_side_effects=True, vmem_limit_bytes=62 * 2**20),
-        cost_estimate=pl.CostEstimate(flops=16 * NX * NH * NC * R * D * F, bytes_accessed=12 * D * F, transcendentals=0),
+        compiler_params=pltpu.CompilerParams(collective_id=0, has_side_effects=True, vmem_limit_bytes=55 * 2**20),
+        cost_estimate=pl.CostEstimate(flops=16 * NX * NH * NC * R * D * F, bytes_accessed=6 * D * F, transcendentals=0),
     )(x, c, wg, wu, wd)
     return tuple(
         pl.pallas_call(
             place,
             name="place_outputs",
             out_shape=out_shape,
-            in_specs=[anywhere] * 4,
+            in_specs=[vmem] * 4,
             out_specs=[anywhere] * 4,
-            scratch_shapes=[pltpu.VMEM(a.shape, BF16) for a in out_shape] + [pltpu.SemaphoreType.DMA((8,))] * 2,
-            compiler_params=pltpu.CompilerParams(vmem_limit_bytes=62 * 2**20),
-            cost_estimate=pl.CostEstimate(flops=0, bytes_accessed=12 * D * F, transcendentals=0),
-        )(*outs)
+            scratch_shapes=[pltpu.SemaphoreType.DMA((4,))],
+            compiler_params=pltpu.CompilerParams(vmem_limit_bytes=2 * 2**20),
+            cost_estimate=pl.CostEstimate(flops=0, bytes_accessed=6 * D * F, transcendentals=0),
+        )(*(pltpu.with_memory_space_constraint(out, pltpu.VMEM) for out in outs))
     )
 
 

time: 111 us -> 106 us (0.955)
  Pallas kernels: 110 us -> 106 us
    pallas_call x1, Pallas kernels: 4.96 us -> 2.52 us  [shards(): pl.pallas_call(place, name='place_outputs', out_shape=out_shape, in_specs...]
    pallas_call x1, Pallas kernels: 105 us -> 103 us  [shards(): pl.pallas_call(body, name='swiglu_block', out_shape=[pltpu.VMEM(a.shape,...]
where the time goes in v4:
time: 106 us
  Pallas kernels  106 us (100%)
    pallas_call x1, Pallas kernels, shards(): pl.pallas_call(body, name='swiglu_block', out_shape=[pltpu.VMEM(a.shape,...  103 us
    pallas_call x1, Pallas kernels, shards(): pl.pallas_call(place, name='place_outputs', out_shape=out_shape, in_specs...  2.52 us

profile of v4, /device:TPU:0, one launch (start us, length us, event | category | flops | bytes accessed | tf_op | source)
XLA Modules:
  0.0 106.4 jit_solution(5077884523309548501)
XLA Ops:
  0.6 103.1 %swiglu_block.1 = (bf16[64,1024]{1,0:T(8,128)(2,1)S(1)}, bf16[1024,896]{1,0:T(8,128)(2,1)S(1)}, bf16[1024,896]{1,0:T(8,128)(2,1)S(1)}, bf16[896,1024]{1,0:T(8,128)(2,1)S(1)}) custom-call(bf16[64,1024]{1,0:T(8,128)(2,1)} %refs_0_.1, bf16[64,1024]{1,0:T(8,128)(2,1)} %refs_1_.1, bf16[1024,896]{1,0:T(8,128)(2,1)} %refs_2_.1, bf16[1024,896]{1,0:T(8,128)(2,1)} %refs_3_.1, ...), custom_call_target="tpu_custom_call" | custom-call | flops 15032385536 | bytes 5505024 | tf_op jit(solution)/shard_map/swiglu_block/pallas_call | solution.py:434
  103.7 2.5 %place_outputs.1 = (bf16[64,1024]{1,0:T(8,128)(2,1)}, bf16[1024,896]{1,0:T(8,128)(2,1)}, bf16[1024,896]{1,0:T(8,128)(2,1)}, bf16[896,1024]{1,0:T(8,128)(2,1)}) custom-call(bf16[64,1024]{1,0:T(8,128)(2,1)S(1)} %get-tuple-element.8.refs_0_, bf16[1024,896]{1,0:T(8,128)(2,1)S(1)} %get-tuple-element.9.refs_1_, bf16[1024,896]{1,0:T(8,128)(2,1)S(1)} %get-tuple-element.10.refs_2_, ...), custom_call_target="tpu_custom_call" | custom-call | bytes 5505024 | tf_op jit(solution)/shard_map/place_outputs/pallas_call | solution.py:445

commit v5 on v4

--- a/solution.py
+++ b/solution.py
@@ -11,17 +11,17 @@
 PLACE = ((0, 0), (0, 1), (1, 0), (3, 0), (1, 1), (3, 1), (2, 0), (2, 1))
 UNITS = ((0,), (1,), (2, 3), (4, 5), (6, 7))
 SPANS = ((0, 2), (2, 4), (4, 6), (6, 8))
-HIDDEN_Y_FIRST = (0, 1, 4)
-DELTAS_Y_FIRST = (0, 1, 2, 3, 4)
+HIDDEN_Y_FIRST = (0, 1, 4,)
+DELTAS_Y_FIRST = (0, 1, 2, 3, 4,)
 CUT = 512
 IN_FLIGHT = 36
 ORDER = (
-    0, 13, 12, 40, 52, 53, 80, 90, 16, 20, 32, 14, 15, 17, 100, 81, 72, 60, 54, 82, 55, 130, 56, 91, 57, 92,
-    33, 102, 83, 73, 34, 132, 93, 112, 84, 74, 103, 122, 94, 104, 113, 142, 114, 152, 134, 133, 124, 110, 162,
-    123, 144, 154, 172, 182, 143, 164, 174, 153, 192, 252, 184, 120, 101, 301, 291, 111, 202, 163, 262, 194,
-    254, 131, 140, 121, 150, 264, 212, 303, 173, 183, 203, 141, 151, 160, 293, 222, 161, 193, 253, 213, 170,
-    171, 200, 292, 180, 263, 181, 201, 210, 242, 204, 223, 302, 190, 250, 191, 211, 251, 214, 221, 290, 260,
-    230, 220, 261, 270, 224, 231, 311, 234, 300, 243, 312, 241, 240, 310, 244, 313, 280,
+    0, 12, 13, 40, 53, 52, 16, 80, 20, 32, 15, 90, 100, 14, 81, 72, 17, 60, 54, 55, 82, 56, 92, 33, 91, 102,
+    57, 83, 34, 130, 73, 112, 132, 84, 93, 74, 122, 103, 94, 104, 142, 152, 114, 162, 134, 124, 113, 111, 172,
+    133, 182, 144, 154, 123, 164, 110, 192, 101, 252, 174, 143, 121, 184, 153, 120, 291, 202, 131, 262, 194,
+    163, 254, 293, 141, 140, 150, 264, 212, 301, 173, 183, 203, 151, 303, 222, 161, 160, 193, 253, 213, 171,
+    170, 201, 302, 181, 263, 180, 200, 211, 242, 204, 223, 311, 191, 251, 210, 190, 250, 214, 261, 221, 300,
+    220, 231, 260, 270, 230, 292, 224, 234, 290, 241, 243, 312, 240, 310, 244, 313, 280,
 )
 
 

time: 106 us -> 105 us (level)
  no operation moved by 1% of the time
where the time goes in v5:
time: 105 us
  Pallas kernels  105 us (100%)
    pallas_call x1, Pallas kernels, shards(): pl.pallas_call(body, name='swiglu_block', out_shape=[pltpu.VMEM(a.shape,...  102 us
    pallas_call x1, Pallas kernels, shards(): pl.pallas_call(place, name='place_outputs', out_shape=out_shape, in_specs...  2.52 us

profile of v5, /device:TPU:0, one launch (start us, length us, event | category | flops | bytes accessed | tf_op | source)
XLA Modules:
  0.0 105.4 jit_solution(14859548905071683780)
XLA Ops:
  0.6 102.0 %swiglu_block.1 = (bf16[64,1024]{1,0:T(8,128)(2,1)S(1)}, bf16[1024,896]{1,0:T(8,128)(2,1)S(1)}, bf16[1024,896]{1,0:T(8,128)(2,1)S(1)}, bf16[896,1024]{1,0:T(8,128)(2,1)S(1)}) custom-call(bf16[64,1024]{1,0:T(8,128)(2,1)} %refs_0_.1, bf16[64,1024]{1,0:T(8,128)(2,1)} %refs_1_.1, bf16[1024,896]{1,0:T(8,128)(2,1)} %refs_2_.1, bf16[1024,896]{1,0:T(8,128)(2,1)} %refs_3_.1, ...), custom_call_target="tpu_custom_call" | custom-call | flops 15032385536 | bytes 5505024 | tf_op jit(solution)/shard_map/swiglu_block/pallas_call | solution.py:434
  102.7 2.5 %place_outputs.1 = (bf16[64,1024]{1,0:T(8,128)(2,1)}, bf16[1024,896]{1,0:T(8,128)(2,1)}, bf16[1024,896]{1,0:T(8,128)(2,1)}, bf16[896,1024]{1,0:T(8,128)(2,1)}) custom-call(bf16[64,1024]{1,0:T(8,128)(2,1)S(1)} %get-tuple-element.8.refs_0_, bf16[1024,896]{1,0:T(8,128)(2,1)S(1)} %get-tuple-element.9.refs_1_, bf16[1024,896]{1,0:T(8,128)(2,1)S(1)} %get-tuple-element.10.refs_2_, ...), custom_call_target="tpu_custom_call" | custom-call | bytes 5505024 | tf_op jit(solution)/shard_map/place_outputs/pallas_call | solution.py:445
